TPU v7x, 32 devices: a whole 2x2x4 slice. The times are simulated.
32 devices in a mesh: groups: 2 (over y), rep: 4 (over z), head: 4 (over x, core).
Axes of the slice: x: 2, y: 2, z: 4, core: 2. Of those that a mesh axis runs over, the one named last changes fastest.
Arguments:
- residual: bfloat16 [32, 5120], P(('groups', 'rep'), 'head'), parts along dimension 0, may hold values from -3 to 3
- queries: bfloat16 [32, 96, 128], P(('groups', 'rep'), 'head'), parts along dimension 0, may hold values from -110 to 110
- cache_keys: bfloat16 [32, 8, 128, 128], P(('groups', 'rep'), 'head'), parts along dimension 0, may hold values from -5 to 5
- cache_values: bfloat16 [32, 8, 128, 128], P(('groups', 'rep'), 'head'), parts along dimension 0, may hold values from -5 to 5
- new_keys: bfloat16 [32, 8, 128], P(('groups', 'rep'), 'head'), parts along dimension 0, may hold values from -5 to 5
- new_values: bfloat16 [32, 8, 128], P(('groups', 'rep'), 'head'), parts along dimension 0, may hold values from -5 to 5
- cache_lengths: int32 [32], P(('groups', 'rep')), parts along dimension 0, may hold values from 1 to 128, as said below
- out_proj: bfloat16 [12288, 5120], P('head', 'rep'), may hold values from -0.21875 to 0.21875
- norm_gain: float32 [5120], replicated, may hold values from 0.25 to 2.5
- skip_flags: int32 [32], P(('groups', 'rep')), parts along dimension 0, may hold values 0 or 1
- expert_ids: int32 [32, 2], P(('groups', 'rep')), parts along dimension 0, may hold values from 0 to 3, all different within a row; in each aligned block of 4 rows (0 to 3, 4 to 7, ...) at most 2 rows name the same one
- route_scores: float32 [32, 2], P(('groups', 'rep')), parts along dimension 0, may hold values from 0.05 to 1
- gate_w: bfloat16 [4, 5120, 1024], P('rep', None, 'head'), may hold values from -0.078125 to 0.078125
- up_w: bfloat16 [4, 5120, 1024], P('rep', None, 'head'), may hold values from -0.078125 to 0.078125
- down_w: bfloat16 [4, 1024, 5120], P('rep', 'head'), may hold values from -0.1875 to 0.1875
Outputs:
- layer_out: bfloat16 [32, 5120], P(('groups', 'rep'), 'head'), parts along dimension 0
There are 2 independent parts, one for each index of `groups`. A program takes and returns all parts, laid end to end along the dimension named above; an argument that names none is the same for every part. Nothing has to cross between parts.
Inputs may be any that keep to these rules, and one draw needn't show every extreme that they name: `cache_lengths`: number of filled cache slots of each row; in every aligned block of 4 rows one row has all 128. `skip_flags`: 1 marks a row that skips the layer. `expert_ids`: each row names 2 different experts; among the 4 rows of one device no expert is named by more than 2 rows, a bound that some block reaches.
All inputs are finite; a program needn't handle non-finite values. No bound on the sum of `skip_flags` on one device may be relied on, other than what follows from the above.
Results may differ from a plain program's by a relative error of at most 0.018.
Values may be sent and summed in bfloat16 or wider, within the bound.
A program may use at most 64 MiB of HBM per device.

v0:
```python
import math

import jax
import jax.numpy as jnp
from jax import lax
from jax.sharding import PartitionSpec as P

D = 5120
CAP = 2


def hidden_block(arrivals, gate_w, up_w):
    gate_part = jnp.einsum("secd,edf->secf", arrivals, gate_w, preferred_element_type=jnp.float32)
    up_part = jnp.einsum("secd,edf->secf", arrivals, up_w, preferred_element_type=jnp.float32)
    return (jax.nn.silu(gate_part) * up_part).astype(jnp.bfloat16)


def per_device(
    residual,
    queries,
    cache_keys,
    cache_values,
    new_keys,
    new_values,
    cache_lengths,
    out_proj,
    norm_gain,
    skip_flags,
    expert_ids,
    route_scores,
    gate_w,
    up_w,
    down_w,
):
    rep_count = lax.axis_size("rep")
    local_rows = residual.shape[0]
    column_block = residual.shape[1]
    kv_local = cache_keys.shape[1]
    head_local = queries.shape[1]
    head_size = queries.shape[2]
    scaling = 1.0 / math.sqrt(head_size)
    grouped = queries.reshape(local_rows, kv_local, head_local // kv_local, head_size)
    scores = (
        jnp.einsum("rkgd,rkpd->rkgp", grouped, cache_keys, preferred_element_type=jnp.float32)
        * scaling
    )
    own_score = (
        jnp.einsum("rkgd,rkd->rkg", grouped, new_keys, preferred_element_type=jnp.float32) * scaling
    )
    filled = jnp.arange(cache_keys.shape[2], dtype=jnp.int32)[None, :] < cache_lengths[:, None]
    scores = jnp.where(filled[:, None, None, :], scores, -jnp.inf)
    highest = jnp.maximum(jnp.max(scores, axis=-1), own_score)
    powers = jnp.exp(scores - highest[..., None])
    own_power = jnp.exp(own_score - highest)
    denominator = jnp.sum(powers, axis=-1) + own_power
    probs = (powers / denominator[..., None]).astype(jnp.bfloat16)
    own_prob = (own_power / denominator).astype(jnp.bfloat16)
    attended = jnp.einsum(
        "rkgp,rkpd->rkgd", probs, cache_values, preferred_element_type=jnp.float32
    )
    attended = (
        attended
        + own_prob.astype(jnp.float32)[..., None] * new_values.astype(jnp.float32)[:, :, None, :]
    )
    attended = attended.astype(jnp.bfloat16).reshape(local_rows, head_local * head_size)
    partial_cols = jnp.dot(
        lax.all_gather(attended, "rep", axis=0, tiled=True),
        out_proj,
        preferred_element_type=jnp.float32,
    )
    regrouped = lax.all_to_all(
        partial_cols.astype(jnp.bfloat16), "rep", split_axis=0, concat_axis=1, tiled=True
    ).astype(partial_cols.dtype)
    projected = lax.psum_scatter(
        regrouped.astype(jnp.bfloat16), "head", scatter_dimension=1, tiled=True
    ).astype(jnp.float32)
    middle = (residual.astype(jnp.float32) + projected).astype(jnp.bfloat16)
    middle_wide = middle.astype(jnp.float32)
    exp_local = gate_w.shape[0]
    experts_all = rep_count * exp_local
    slot_count = experts_all * CAP
    top_count = expert_ids.shape[1]
    live = skip_flags == 0
    choose = (
        (expert_ids[:, :, None] == jnp.arange(experts_all, dtype=jnp.int32)[None, None, :])
        & live[:, None, None]
    ).astype(jnp.int32)
    flat_hits = choose.reshape(local_rows * top_count, experts_all)
    before = jnp.cumsum(flat_hits, axis=0) - flat_hits
    rank = jnp.sum(before * flat_hits, axis=1).reshape(local_rows, top_count)
    target = jnp.where(live[:, None], expert_ids * CAP + rank, -1)
    marks = (target[:, :, None] == jnp.arange(slot_count, dtype=jnp.int32)[None, None, :]).astype(
        jnp.float32
    )
    placing = jnp.sum(marks, axis=1).astype(jnp.bfloat16)
    shares = (route_scores / jnp.sum(route_scores, axis=1, keepdims=True)).astype(jnp.bfloat16)
    combine = jnp.sum(marks * shares.astype(jnp.float32)[:, :, None], axis=1).astype(jnp.bfloat16)
    full_middle = lax.all_gather(middle, "head", axis=1, tiled=True).astype(jnp.float32)
    mean_square = jnp.mean(full_middle * full_middle, axis=-1, keepdims=True)
    normed = (full_middle * lax.rsqrt(mean_square + 1e-05) * norm_gain[None, :]).astype(
        jnp.bfloat16
    )
    outgoing = jnp.einsum("rs,rd->sd", placing, normed, preferred_element_type=jnp.float32).astype(
        jnp.bfloat16
    )
    outgoing = outgoing.reshape(rep_count, exp_local, CAP, D)
    hidden = hidden_block(
        lax.all_to_all(outgoing, "rep", split_axis=0, concat_axis=0, tiled=True), gate_w, up_w
    )
    partial_out = jnp.einsum("secf,efd->secd", hidden, down_w, preferred_element_type=jnp.float32)
    summed = lax.psum_scatter(
        partial_out.astype(jnp.bfloat16), "head", scatter_dimension=3, tiled=True
    )
    expert_out = lax.all_to_all(summed, "rep", split_axis=0, concat_axis=0, tiled=True)
    expert_out = expert_out.reshape(slot_count, column_block)
    mixed = jnp.dot(combine, expert_out, preferred_element_type=jnp.float32)
    result = jnp.where(live[:, None], middle_wide + mixed, residual.astype(jnp.float32))
    return result.astype(jnp.bfloat16)


def solution(mesh):
    return jax.shard_map(
        per_device,
        mesh=mesh,
        in_specs=(
            P(("groups", "rep"), "head"),
            P(("groups", "rep"), "head", None),
            P(("groups", "rep"), "head", None, None),
            P(("groups", "rep"), "head", None, None),
            P(("groups", "rep"), "head", None),
            P(("groups", "rep"), "head", None),
            P(("groups", "rep")),
            P("head", "rep"),
            P(),
            P(("groups", "rep")),
            P(("groups", "rep"), None),
            P(("groups", "rep"), None),
            P("rep", None, "head"),
            P("rep", None, "head"),
            P("rep", "head", None),
        ),
        out_specs=P(("groups", "rep"), "head"),
        check_vma=False,
    )
```

profile of v0, /device:TPU:0, one launch (start us, length us, event | category | flops | bytes accessed | tf_op | source)
XLA Modules:
  0.0 144.9 jit_solution(15133338549335284825)
XLA Ops:
  6.5 0.0 copy-start
  6.5 0.9 iota_compare_fusion.2
  7.4 0.7 convert_element_type.83
  8.1 0.7 copy.35
  8.8 0.8 fusion.40
  9.7 1.3 fusion.59
  11.0 0.2 fusion.36
  11.2 1.2 fusion.9
  12.4 15.0 %all-gather = bf16[4,4,3072]{2,1,0:T(4,128)(2,1)S(1)} all-gather(bf16[1,4,3072]{2,1,0:T(4,128)(2,1)S(1)} %reshape.88), channel_id=1, replica_groups=mesh['groups'=2,'rep'=4,'head'=4] {'rep'}, dimensions={0}, use_global_device_ids=true | all-gather | bytes 122880 | tf_op jit(solution)/shard_map/all_gather | solution.py:67
  27.5 0.0 copy-start.5
  27.5 0.0 copy-start.3
  27.5 0.0 copy-start.2
  27.5 4.4 %convolution_convert_fusion.2 = bf16[16,1280]{1,0:T(8,128)(2,1)S(1)} fusion(bf16[16,3072]{1,0:T(8,128)(2,1)S(1)} %reshape.89, bf16[3072,1280]{1,0:T(8,128)(2,1)} %param.22), kind=kOutput, calls=%fused_computation.8 | convolution fusion | flops 125849600 | bytes 8003584 | tf_op jit(solution)/shard_map/dot_general | solution.py:66
  31.9 0.0 copy-start.1
  31.9 0.0 copy-start.4
  31.9 0.6 all_to_all.20
  32.5 4.7 %all-to-all-start = ((bf16[4,4,1280]{2,1,0:T(4,128)(2,1)}), bf16[4,4,1280]{2,1,0:T(4,128)(2,1)S(1)}, u32[]{:S(2)}, u32[]{:S(2)}) async-start(bf16[4,4,1280]{2,1,0:T(4,128)(2,1)} %all_to_all.20), calls=%async_computation | async-start | bytes 81920 | tf_op jit(solution)/shard_map/all_to_all | solution.py:71
  37.2 0.0 reduce-scatter.7.cloned.1.call-start
  37.3 0.0 copy-done.5
  37.3 0.1 broadcast_in_dim.32
  37.3 0.1 and.11
  37.4 0.0 copy-done.3
  37.4 0.1 copy.37
  37.5 0.1 eq.33
  37.6 0.2 reduce_window_sum.11
  37.8 0.1 reshape.80
  37.9 0.1 add_select_fusion
  38.0 0.0 copy-done.2
  38.0 0.1 copy.39
  38.1 4.8 %all-to-all-done = bf16[4,4,1280]{2,1,0:T(4,128)(2,1)S(1)} async-done(((bf16[4,4,1280]{2,1,0:T(4,128)(2,1)}), bf16[4,4,1280]{2,1,0:T(4,128)(2,1)S(1)}, u32[]{:S(2)}, u32[]{:S(2)}) %all-to-all-start) | async-done | bytes 40992 | tf_op jit(solution)/shard_map/all_to_all | solution.py:71
  42.9 1.6 %copy.45 = bf16[4,5120]{0,1:T(8,128)(2,1)} copy(bf16[4,5120]{1,0:T(4,128)(2,1)S(1)} %bitcast.85) | data formatting | bytes 81920
  44.5 0.0 reduce-scatter.7.cloned.1.call-update
  44.5 0.0 reduce-scatter.9.cloned.1.call-start
  44.6 0.1 select_reduce_fusion
  44.6 25.0 %reduce-scatter.7.cloned.1.call-done = bf16[1280,4]{1,0:T(8,128)(2,1)} async-done(((bf16[5120,4]{1,0:T(8,128)(2,1)}), bf16[1280,4]{1,0:T(8,128)(2,1)}) %reduce-scatter.7.cloned.1.call-update) | async-done | bytes 10256
  69.6 1.1 copy.46
  70.8 0.0 copy-done.1
  70.8 5.2 %all_gather.7 = bf16[4,5120]{1,0:T(4,128)(2,1)S(1)} all-gather(bf16[4,1280]{1,0:T(4,128)(2,1)S(1)} %fusion.45), channel_id=1, replica_groups=mesh['groups'=2,'rep'=4,'head'=4] {'head'}, dimensions={1}, use_global_device_ids=true | all-gather | bytes 51200 | tf_op jit(solution)/shard_map/all_gather | solution.py:98
  76.0 0.2 fusion.27
  76.2 0.0 copy-done.4
  76.2 0.2 convolution_convert_fusion.1
  76.5 10.2 %all_to_all.29 = bf16[4,1,2,5120]{3,2,1,0:T(2,128)(2,1)S(1)} all-to-all(bf16[4,1,2,5120]{3,2,1,0:T(2,128)(2,1)S(1)} %bitcast.84), channel_id=1, replica_groups=mesh['groups'=2,'rep'=4,'head'=4] {'rep'}, dimensions={0} | all-to-all | bytes 163840 | tf_op jit(solution)/shard_map/all_to_all | solution.py:108
  86.6 2.2 %fusion.10 = f32[4,1,2,256]{3,0,2,1:T(4,128)S(1)} fusion(bf16[1,5120,256]{2,1,0:T(8,128)(2,1)} %param.27, bf16[4,1,2,5120]{3,2,1,0:T(2,128)(2,1)S(1)} %all_to_all.29), kind=kOutput, calls=%fused_computation.16 | convolution fusion | flops 20971520 | bytes 2711552 | tf_op jit(solution)/shard_map/secd,edf->secf/dot_general | solution.py:13
  88.9 0.0 copy-done
  88.9 2.7 %fusion = bf16[4,1,2,5120]{3,0,2,1:T(4,128)(2,1)S(1)} fusion(bf16[1,256,5120]{2,1,0:T(8,128)(2,1)S(1)} %copy-done, bf16[1,5120,256]{2,1,0:T(8,128)(2,1)} %param.28, bf16[4,1,2,5120]{3,2,1,0:T(2,128)(2,1)S(1)} %all_to_all.29, f32[4,1,2,256]{3,0,2,1:T(4,128)S(1)} %fusion.10), kind=kOutput, calls=%fused_computation.2 | convolution fusion | flops 41996288 | bytes 5414912 | tf_op jit(solution)/shard_map/secf,efd->secd/dot_general | solution.py:110
  91.5 4.2 %copy.47 = bf16[4,1,2,5120]{0,2,1,3:T(2,128)(2,1)} copy(bf16[4,1,2,5120]{3,0,2,1:T(4,128)(2,1)S(1)} %fusion) | data formatting | bytes 163840
  95.7 5.4 %reshape.98 = bf16[5120,8]{1,0:T(8,128)(2,1)} reshape(bf16[5120,1,2,4]{3,2,1,0:T(2,128)(2,1)} %bitcast.80) | data formatting | bytes 163840
  101.0 0.0 reduce-scatter.9.cloned.1.call-update
  101.1 24.5 %reduce-scatter.9.cloned.1.call-done = bf16[1280,8]{1,0:T(8,128)(2,1)} async-done(((bf16[5120,8]{1,0:T(8,128)(2,1)}), bf16[1280,8]{1,0:T(8,128)(2,1)}) %reduce-scatter.9.cloned.1.call-update) | async-done | bytes 20496
  125.6 1.3 reshape.99
  126.8 0.4 copy.42
  127.3 10.0 %all_to_all.30 = bf16[4,1,2,1280]{3,2,1,0:T(2,128)(2,1)S(1)} all-to-all(bf16[4,1,2,1280]{3,2,1,0:T(2,128)(2,1)S(1)} %copy.42), channel_id=1, replica_groups=mesh['groups'=2,'rep'=4,'head'=4] {'rep'}, dimensions={0} | all-to-all | bytes 40960 | tf_op jit(solution)/shard_map/all_to_all | solution.py:114
  137.3 0.7 fusion.7
  (13 shorter events, 0.2 us)
Async XLA Ops:
  6.5 82.3 %copy-start = (bf16[1,256,5120]{2,1,0:T(8,128)(2,1)S(1)}, bf16[1,256,5120]{2,1,0:T(8,128)(2,1)}, u32[]{:S(2)}) copy-start(bf16[1,256,5120]{2,1,0:T(8,128)(2,1)} %param.29) | copy-start | bytes 7864324
  27.5 9.8 %copy-start.5 = (s32[4]{0:T(128)S(1)}, s32[4]{0:T(128)}, u32[]{:S(2)}) copy-start(s32[4]{0:T(128)} %param.24) | copy-start | bytes 52
  27.5 9.9 %copy-start.3 = (s32[4,2]{0,1:T(2,128)S(1)}, s32[4,2]{0,1:T(2,128)}, u32[]{:S(2)}) copy-start(s32[4,2]{0,1:T(2,128)} %param.25) | copy-start | bytes 100
  27.5 10.5 %copy-start.2 = (f32[4,2]{0,1:T(2,128)S(1)}, f32[4,2]{0,1:T(2,128)}, u32[]{:S(2)}) copy-start(f32[4,2]{0,1:T(2,128)} %param.26) | copy-start | bytes 100
  31.9 38.9 %copy-start.1 = (bf16[4,1280]{1,0:T(4,128)(2,1)S(1)}, bf16[4,1280]{1,0:T(4,128)(2,1)}, u32[]{:S(2)}) copy-start(bf16[4,1280]{1,0:T(4,128)(2,1)} %param.15) | copy-start | bytes 30724
  31.9 44.3 %copy-start.4 = (f32[5120]{0:T(1024)S(1)}, f32[5120]{0:T(1024)}, u32[]{:S(2)}) copy-start(f32[5120]{0:T(1024)} %param.23) | copy-start | bytes 61444
  32.5 10.4 %all-to-all-start = ((bf16[4,4,1280]{2,1,0:T(4,128)(2,1)}), bf16[4,4,1280]{2,1,0:T(4,128)(2,1)S(1)}, u32[]{:S(2)}, u32[]{:S(2)}) async-start(bf16[4,4,1280]{2,1,0:T(4,128)(2,1)} %all_to_all.20), calls=%async_computation | async-start | bytes 81920 | tf_op jit(solution)/shard_map/all_to_all | solution.py:71
  37.2 32.4 %reduce-scatter.7.cloned.1.call-start = ((), (), s32[]{:S(2)}) async-start(), calls=%async_computation.5 | async-start | bytes 1638400
  44.5 81.0 %reduce-scatter.9.cloned.1.call-start = ((), (), s32[]{:S(2)}) async-start(), calls=%async_computation.6 | async-start | bytes 1638400
Sparse Core Ops, SparseCore 0:
  44.6 24.9 reduce-scatter.6
  101.2 24.3 reduce-scatter.8
where the time goes:
time: 146 us; the launch traced here: 145 us
  waiting for transfers between devices  54.3 us (37%)
  blocking collectives  40.5 us (28%)
  local copies, waits for them, and re-layouts  16 us (11%)
  matrix products  13.5 us (9%)
  between operations  13.5 us (9%)
  starting transfers between devices  4.77 us (3%)
  other arithmetic  2.38 us (2%)
    unnamed x4, waiting for transfers between devices  49.5 us
    all_gather x1, blocking collectives, per_device(): lax.all_gather(attended, 'rep', axis=0, tiled=True)  15 us
    unnamed x21, local copies, waits for them, and re-layouts  14.4 us
    all_to_all x1, blocking collectives, per_device(): lax.all_to_all(outgoing, 'rep', split_axis=0, concat_axis=0, tiled=True)  10.2 us
    all_to_all x1, blocking collectives, per_device(): lax.all_to_all(summed, 'rep', split_axis=0, concat_axis=0, tiled=True)  10 us
    all_gather x1, blocking collectives, per_device(): lax.all_gather(middle, 'head', axis=1, tiled=True).astype(jnp.float32)  5.22 us
    all_to_all x1, waiting for transfers between devices, per_device(): lax.all_to_all(partial_cols.astype(jnp.bfloat16), 'rep', split_axis=0, co...  4.82 us
    all_to_all x1, starting transfers between devices, per_device(): lax.all_to_all(partial_cols.astype(jnp.bfloat16), 'rep', split_axis=0, co...  4.72 us
  transfers between devices with their start and end apart: 3, of which 3 were waited for; matrix products, arithmetic and copies ran while one was open for 1% of the time, Pallas kernels for 0%

commit v1 on v0

--- a/solution.py
+++ b/solution.py
@@ -3,6 +3,8 @@
 import jax
 import jax.numpy as jnp
 from jax import lax
+from jax.experimental import pallas as pl
+from jax.experimental.pallas import tpu as pltpu
 from jax.sharding import PartitionSpec as P
 
 D = 5120
@@ -118,9 +120,550 @@
     return result.astype(jnp.bfloat16)
 
 
+MESH = pl.DeviceIdType.MESH
+N = 4
+ROWS = 4
+ALL = N * ROWS
+HEAD_SIZE = 128
+PIECE = 384
+STARTS = (0, 384, 768, 1024)
+WIDTHS = (384, 384, 256, 256)
+
+
+def fits_fused(mesh):
+    return mesh.shape["rep"] == N and mesh.shape["head"] == N
+
+
+def pack_rows(x):
+    pieces = []
+    for start, width in zip(STARTS, WIDTHS):
+        piece = x[:, start : start + width]
+        if width < PIECE:
+            piece = jnp.concatenate(
+                [piece, jnp.zeros((x.shape[0], PIECE - width), x.dtype)], axis=1
+            )
+        pieces.append(piece)
+    return jnp.concatenate(pieces, axis=0)
+
+
+def unpack_rows(y):
+    return jnp.concatenate(
+        [y[ROWS * i : ROWS * (i + 1), :width] for i, width in enumerate(WIDTHS)], axis=1
+    )
+
+
+def by_row(shape, group, read):
+    row = lax.broadcasted_iota(jnp.int32, shape, 0) // group
+    out = jnp.full(shape, read(0))
+    for i in range(1, shape[0] // group):
+        out = jnp.where(row == i, read(i), out)
+    return out
+
+
+def dot(a, b):
+    return jnp.dot(a, b, preferred_element_type=jnp.float32)
+
+
+def fused_kernel(
+    queries,
+    cache_keys,
+    cache_values,
+    new_keys,
+    new_values,
+    residual,
+    out_proj,
+    norm_gain,
+    gate_w,
+    up_w,
+    down_w,
+    lengths,
+    skips,
+    ids,
+    routes,
+    out,
+    q_v,
+    k_v,
+    v_v,
+    nk_v,
+    nv_v,
+    res_v,
+    w_v,
+    gain_v,
+    gate_v,
+    up_v,
+    down_v,
+    att_f,
+    att_all,
+    att_wide,
+    res_pack,
+    res_in,
+    proj_out,
+    proj_in,
+    mid_all,
+    exp_out,
+    exp_in,
+    back_out,
+    back_in,
+    load_sem,
+    w_sem,
+    att_send,
+    att_recv,
+    res_send,
+    res_recv,
+    proj_send,
+    proj_recv,
+    mid_send,
+    fwd_send,
+    mid_recv,
+    exp_send,
+    exp_recv,
+    back_send,
+    back_recv,
+):
+    g = lax.axis_index("groups")
+    r = lax.axis_index("rep")
+    h = lax.axis_index("head")
+
+    def remote(src, dst, send, recv, to_rep, to_head):
+        return pltpu.make_async_remote_copy(
+            src_ref=src,
+            dst_ref=dst,
+            send_sem=send,
+            recv_sem=recv,
+            device_id=(g, to_rep, to_head),
+            device_id_type=MESH,
+        )
+
+    barrier = pltpu.get_barrier_semaphore()
+    for i in range(N):
+        for j in range(N):
+
+            @pl.when(jnp.logical_or(r != i, h != j))
+            def _():
+                pl.semaphore_signal(barrier, inc=1, device_id=(g, i, j), device_id_type=MESH)
+
+    loads = [
+        pltpu.make_async_copy(src, dst, load_sem.at[i])
+        for i, (src, dst) in enumerate(
+            (
+                (queries, q_v),
+                (cache_keys, k_v),
+                (new_keys, nk_v),
+                (new_values, nv_v),
+                (residual, res_v),
+                (cache_values, v_v),
+                (norm_gain, gain_v),
+                (gate_w, gate_v),
+                (up_w, up_v),
+                (down_w, down_v),
+            )
+        )
+    ]
+    depth = w_v.shape[0] // N
+    w_loads = [
+        pltpu.make_async_copy(
+            out_proj.at[pl.ds(c * depth, depth)], w_v.at[pl.ds(c * depth, depth)], w_sem.at[c]
+        )
+        for c in range(N)
+    ]
+    for copy in loads[:6]:
+        copy.start()
+    for copy in w_loads:
+        copy.start()
+    for copy in loads[6:]:
+        copy.start()
+
+    heads = q_v.shape[1]
+    kv = k_v.shape[1]
+    lines = ROWS * heads
+    blocks = ROWS * kv
+    per_block = heads // kv
+    scaling = 1.0 / math.sqrt(HEAD_SIZE)
+    loads[0].wait()
+    q = q_v[...].astype(jnp.float32).reshape(lines, HEAD_SIZE).astype(jnp.bfloat16)
+    loads[1].wait()
+    keys = k_v[...].reshape(blocks * k_v.shape[2], HEAD_SIZE)
+    slots = k_v.shape[2]
+    wide = lax.dot_general(
+        q, keys, (((1,), (1,)), ((), ())), preferred_element_type=jnp.float32
+    )
+    block = lax.broadcasted_iota(jnp.int32, (lines, slots), 0) // per_block
+    scores = wide[:, :slots]
+    for t in range(1, blocks):
+        scores = jnp.where(block == t, wide[:, t * slots : (t + 1) * slots], scores)
+    scores = scores * scaling
+    loads[2].wait()
+    loads[3].wait()
+    nk = jnp.concatenate([nk_v[i].astype(jnp.float32) for i in range(ROWS)], axis=0)
+    nv = jnp.concatenate([nv_v[i].astype(jnp.float32) for i in range(ROWS)], axis=0)
+    own_wide = lax.dot_general(
+        q, nk.astype(jnp.bfloat16), (((1,), (1,)), ((), ())), preferred_element_type=jnp.float32
+    )
+    own_here = lax.broadcasted_iota(
+        jnp.int32, (lines, blocks), 0
+    ) // per_block == lax.broadcasted_iota(jnp.int32, (lines, blocks), 1)
+    own = jnp.sum(jnp.where(own_here, own_wide, 0.0), axis=1, keepdims=True) * scaling
+    filled = lax.broadcasted_iota(jnp.int32, (lines, slots), 1) < by_row(
+        (lines, slots), heads, lambda i: lengths[i]
+    )
+    scores = jnp.where(filled, scores, -jnp.inf)
+    highest = jnp.maximum(jnp.max(scores, axis=1, keepdims=True), own)
+    powers = jnp.exp(scores - highest)
+    own_power = jnp.exp(own - highest)
+    denominator = jnp.sum(powers, axis=1, keepdims=True) + own_power
+    probs = powers / denominator
+    own_prob = own_power / denominator
+    spread = jnp.concatenate(
+        [jnp.where(block == t, probs, 0.0).astype(jnp.bfloat16) for t in range(blocks)], axis=1
+    )
+    own_spread = jnp.where(own_here, own_prob, 0.0).astype(jnp.bfloat16)
+    loads[5].wait()
+    att = dot(spread, v_v[...].reshape(blocks * slots, HEAD_SIZE))
+    att_f[...] = att + dot(own_spread, nv.astype(jnp.bfloat16))
+    per_quarter = heads // N
+    att_all[r] = jnp.concatenate(
+        [att_f[pl.ds(j, ALL, stride=per_quarter), :] for j in range(per_quarter)], axis=1
+    ).astype(jnp.bfloat16)
+    loads[4].wait()
+    res = res_v[...].astype(jnp.float32)
+    res_pack[...] = pack_rows(res).astype(jnp.bfloat16)
+
+    pl.semaphore_wait(barrier, N * N - 1)
+
+    def att_copy(i):
+        return remote(att_all.at[r], att_all.at[r], att_send.at[i], att_recv.at[r], i, h)
+
+    def att_arrival(i):
+        return remote(att_all.at[i], att_all.at[i], att_send.at[i], att_recv.at[i], i, h)
+
+    def res_copy(j):
+        return remote(res_pack, res_in.at[r], res_send.at[j], res_recv.at[r], h, j)
+
+    def res_arrival(i):
+        return remote(res_pack, res_in.at[i], res_send.at[i], res_recv.at[i], i, r)
+
+    for i in range(N):
+
+        @pl.when(r != i)
+        def _():
+            att_copy(i).start()
+
+    for j in range(N):
+
+        @pl.when(jnp.logical_or(r != h, h != j))
+        def _():
+            res_copy(j).start()
+
+    @pl.when(r == h)
+    def _():
+        res_in[r] = res_pack[...]
+
+    for i in range(N):
+
+        @pl.when(r != i)
+        def _():
+            att_arrival(i).wait_recv()
+
+    for t in range(per_quarter):
+        cut = att_all[:, :, t * HEAD_SIZE : (t + 1) * HEAD_SIZE]
+        att_wide[t] = cut.astype(jnp.float32).reshape(N * ALL, HEAD_SIZE)
+    total = None
+    for c in range(N):
+        w_loads[c].wait()
+        lhs = jnp.concatenate(
+            [att_wide[t, pl.ds(c, ALL, stride=N), :] for t in range(per_quarter)], axis=1
+        ).astype(jnp.bfloat16)
+        part = dot(lhs, w_v[pl.ds(c * depth, depth), :])
+        total = part if total is None else total + part
+
+    def proj_copy(j):
+        return remote(proj_out.at[j], proj_in.at[h], proj_send.at[j], proj_recv.at[h], r, j)
+
+    def proj_arrival(j):
+        return remote(proj_out.at[j], proj_in.at[j], proj_send.at[j], proj_recv.at[j], r, j)
+
+    for j in range(N):
+        piece = total[:, STARTS[j] : STARTS[j] + WIDTHS[j]].astype(jnp.bfloat16)
+        proj_out[j, :, : WIDTHS[j]] = piece
+        if WIDTHS[j] < PIECE:
+            proj_out[j, :, WIDTHS[j] :] = jnp.zeros((ALL, PIECE - WIDTHS[j]), jnp.bfloat16)
+
+        @pl.when(h != j)
+        def _():
+            proj_copy(j).start()
+
+        @pl.when(h == j)
+        def _():
+            proj_in[j] = proj_out[j]
+
+    for i in range(N):
+
+        @pl.when(jnp.logical_or(r != h, r != i))
+        def _():
+            res_arrival(i).wait_recv()
+
+    res_all = [res_in[i].astype(jnp.float32) for i in range(N)]
+    middle = jnp.zeros((ALL, PIECE), jnp.float32)
+    for j in range(N):
+        mine = jnp.concatenate([x[ROWS * j : ROWS * (j + 1)] for x in res_all], axis=0)
+        middle = jnp.where(h == j, mine, middle)
+    for j in range(N):
+
+        @pl.when(h != j)
+        def _():
+            proj_arrival(j).wait_recv()
+
+    summed = proj_in[0].astype(jnp.float32)
+    for j in range(1, N):
+        summed = summed + proj_in[j].astype(jnp.float32)
+    mid_all[r, h] = (middle + summed).astype(jnp.bfloat16)
+
+    def mid_copy(i):
+        return remote(
+            mid_all.at[r, h], mid_all.at[r, h], mid_send.at[i], mid_recv.at[r, h], i, h
+        )
+
+    def mid_arrival(i, j):
+        return remote(
+            mid_all.at[i, j], mid_all.at[i, j], mid_send.at[i], mid_recv.at[i, j], i, j
+        )
+
+    def mid_forward(i, j):
+        return remote(
+            mid_all.at[i, h], mid_all.at[i, h], fwd_send.at[i, j], mid_recv.at[i, h], r, j
+        )
+
+    for i in range(N):
+
+        @pl.when(r != i)
+        def _():
+            mid_copy(i).start()
+
+    for j in range(N):
+
+        @pl.when(h != j)
+        def _():
+            mid_forward(r, j).start()
+
+    for i in range(N):
+
+        @pl.when(r != i)
+        def _():
+            mid_arrival(i, h).wait_recv()
+            for j in range(N):
+
+                @pl.when(h != j)
+                def _():
+                    mid_forward(i, j).start()
+
+    for i in range(6, 10):
+        loads[i].wait()
+    for i in range(N):
+        for j in range(N):
+
+            @pl.when(h != j)
+            def _():
+                mid_arrival(i, j).wait_recv()
+
+    rows = []
+    squares = jnp.zeros((ALL, 1), jnp.float32)
+    for i in range(N):
+        x = jnp.concatenate([mid_all[i, j][:, : WIDTHS[j]] for j in range(N)], axis=1).astype(
+            jnp.float32
+        )
+        rows.append(x)
+        squares = squares + jnp.sum(x * x, axis=1, keepdims=True)
+    columns = rows[0].shape[1]
+    scale = lax.rsqrt(squares * (1.0 / (N * columns)) + 1e-05)
+    gate = jnp.zeros((ALL, gate_v.shape[2]), jnp.float32)
+    up = jnp.zeros((ALL, up_v.shape[2]), jnp.float32)
+    for i in range(N):
+        cut = pl.ds(i * columns, columns)
+        normed = (rows[i] * scale * gain_v[:, cut]).astype(jnp.bfloat16)
+        gate = gate + dot(normed, gate_v[0, cut, :])
+        up = up + dot(normed, up_v[0, cut, :])
+    hidden = (gate / (1.0 + jnp.exp(-gate)) * up).astype(jnp.bfloat16)
+
+    def exp_copy(j):
+        return remote(exp_out.at[j], exp_in.at[h], exp_send.at[j], exp_recv.at[h], r, j)
+
+    def exp_arrival(j):
+        return remote(exp_out.at[j], exp_in.at[j], exp_send.at[j], exp_recv.at[j], r, j)
+
+    for j in range(N):
+        exp_out[j] = dot(hidden, down_v[0, :, pl.ds(j * columns, columns)]).astype(jnp.bfloat16)
+
+        @pl.when(h != j)
+        def _():
+            exp_copy(j).start()
+
+        @pl.when(h == j)
+        def _():
+            exp_in[j] = exp_out[j]
+
+    line = lax.broadcasted_iota(jnp.int32, (ROWS, ALL), 1)
+    want = lax.broadcasted_iota(jnp.int32, (ROWS, ALL), 0) + r * ROWS
+    pick = jnp.where(line == want, 1.0, 0.0).astype(jnp.bfloat16)
+    mine = jnp.concatenate([mid_all[h, j][:, : WIDTHS[j]] for j in range(N)], axis=1)
+    own_mid = dot(pick, mine)
+    top = ids.shape[0]
+    packed = (ALL, PIECE)
+    place = lax.broadcasted_iota(jnp.int32, packed, 0) % ROWS
+
+    def spread_rows(read):
+        result = jnp.full(packed, read(0))
+        for i in range(1, ROWS):
+            result = jnp.where(place == i, read(i), result)
+        return result
+
+    scored = [spread_rows(lambda i, k=k: routes[k, i]) for k in range(top)]
+    named = [spread_rows(lambda i, k=k: ids[k, i]) for k in range(top)]
+    whole = sum(scored[1:], scored[0])
+    shares = [(s / whole).astype(jnp.bfloat16).astype(jnp.float32) for s in scored]
+    weights = [
+        sum(jnp.where(named[k] == e, shares[k], 0.0) for k in range(top)) for e in range(N)
+    ]
+
+    for j in range(N):
+
+        @pl.when(h != j)
+        def _():
+            exp_arrival(j).wait_recv()
+
+    expert = exp_in[0].astype(jnp.float32)
+    for j in range(1, N):
+        expert = expert + exp_in[j].astype(jnp.float32)
+
+    def back_copy(i):
+        return remote(back_out.at[i], back_in.at[r], back_send.at[i], back_recv.at[r], i, h)
+
+    def back_arrival(i):
+        return remote(back_out.at[i], back_in.at[i], back_send.at[i], back_recv.at[i], i, h)
+
+    for i in range(N):
+        back_out[i] = pack_rows(expert[ROWS * i : ROWS * (i + 1)]).astype(jnp.bfloat16)
+
+        @pl.when(r != i)
+        def _():
+            back_copy(i).start()
+
+        @pl.when(r == i)
+        def _():
+            back_in[i] = back_out[i]
+
+    for i in range(N):
+
+        @pl.when(r != i)
+        def _():
+            back_arrival(i).wait_recv()
+
+    mixed = weights[0] * back_in[0].astype(jnp.float32)
+    for e in range(1, N):
+        mixed = mixed + weights[e] * back_in[e].astype(jnp.float32)
+    skipped = by_row((ROWS, columns), 1, lambda i: skips[i])
+    out[...] = jnp.where(skipped == 0, own_mid + unpack_rows(mixed), res).astype(jnp.bfloat16)
+
+    for i in range(N):
+
+        @pl.when(r != i)
+        def _():
+            att_copy(i).wait_send()
+            mid_copy(i).wait_send()
+            back_copy(i).wait_send()
+
+        @pl.when(h != i)
+        def _():
+            proj_copy(i).wait_send()
+            exp_copy(i).wait_send()
+            for k in range(N):
+                mid_forward(k, i).wait_send()
+
+        @pl.when(jnp.logical_or(r != h, h != i))
+        def _():
+            res_copy(i).wait_send()
+
+
+def fused_device(
+    residual,
+    queries,
+    cache_keys,
+    cache_values,
+    new_keys,
+    new_values,
+    cache_lengths,
+    out_proj,
+    norm_gain,
+    skip_flags,
+    expert_ids,
+    route_scores,
+    gate_w,
+    up_w,
+    down_w,
+):
+    bf16, f32 = jnp.bfloat16, jnp.float32
+    gain = norm_gain[None, :]
+    inputs = (
+        queries,
+        cache_keys,
+        cache_values,
+        new_keys,
+        new_values,
+        residual,
+        out_proj,
+        gain,
+        gate_w,
+        up_w,
+        down_w,
+    )
+    heads = queries.shape[1]
+    columns = residual.shape[1]
+    depth = heads * HEAD_SIZE // N
+    dma = pltpu.SemaphoreType.DMA
+    return pl.pallas_call(
+        fused_kernel,
+        out_shape=jax.ShapeDtypeStruct(residual.shape, bf16),
+        in_specs=[pl.BlockSpec(memory_space=pl.ANY)] * len(inputs)
+        + [pl.BlockSpec(memory_space=pltpu.SMEM)] * 4,
+        out_specs=pl.BlockSpec(memory_space=pltpu.VMEM),
+        scratch_shapes=[pltpu.VMEM(x.shape, x.dtype) for x in inputs]
+        + [
+            pltpu.VMEM((ROWS * heads, HEAD_SIZE), f32),
+            pltpu.VMEM((N, ALL, depth), bf16),
+            pltpu.VMEM((depth // HEAD_SIZE, N * ALL, HEAD_SIZE), f32),
+            pltpu.VMEM((ALL, PIECE), bf16),
+            pltpu.VMEM((N, ALL, PIECE), bf16),
+            pltpu.VMEM((N, ALL, PIECE), bf16),
+            pltpu.VMEM((N, ALL, PIECE), bf16),
+            pltpu.VMEM((N, N, ALL, PIECE), bf16),
+            pltpu.VMEM((N, ALL, columns), bf16),
+            pltpu.VMEM((N, ALL, columns), bf16),
+            pltpu.VMEM((N, ALL, PIECE), bf16),
+            pltpu.VMEM((N, ALL, PIECE), bf16),
+            dma((10,)),
+            dma((N,)),
+            dma((N,)),
+            dma((N,)),
+            dma((N,)),
+            dma((N,)),
+            dma((N,)),
+            dma((N,)),
+            dma((N,)),
+            dma((N, N)),
+            dma((N, N)),
+            dma((N,)),
+            dma((N,)),
+            dma((N,)),
+            dma((N,)),
+        ],
+        compiler_params=pltpu.CompilerParams(
+            collective_id=0, has_side_effects=True, vmem_limit_bytes=63 * 1024 * 1024
+        ),
+    )(*inputs, cache_lengths, skip_flags, expert_ids.T, route_scores.T)
+
+
 def solution(mesh):
     return jax.shard_map(
-        per_device,
+        fused_device if fits_fused(mesh) else per_device,
         mesh=mesh,
         in_specs=(
             P(("groups", "rep"), "head"),

time: 146 us -> 33.3 us (0.23)
  waiting for transfers between devices: 54.3 us -> 0 us
  blocking collectives: 40.5 us -> 0 us
  Pallas kernels: 0 us -> 31.8 us
  local copies, waits for them, and re-layouts: 16 us -> 1.31 us
  matrix products: 13.5 us -> 0 us
  between operations: 13.5 us -> 0.01 us
  starting transfers between devices: 4.77 us -> 0 us
  other arithmetic: 2.38 us -> 0 us
    unnamed x4 -> x0, waiting for transfers between devices: 49.5 us -> none
    pallas_call x0 -> x1, Pallas kernels: none -> 31.8 us  [fused_device(): pl.pallas_call(fused_kernel, out_shape=jax.ShapeDtypeStruct(residual.shap...]
    all_gather x2 -> x0, blocking collectives: 20.3 us -> none  [the longest x1 15 us: per_device(): lax.all_gather(attended, 'rep', axis=0, tiled=True)]
    all_to_all x2 -> x0, blocking collectives: 20.2 us -> none  [the longest x1 10.2 us: per_device(): lax.all_to_all(outgoing, 'rep', split_axis=0, concat_axis=0, tiled=True)]
    dot_general x8 -> x0, matrix products: 13.5 us -> none  [the longest x1 4.37 us: per_device(): jnp.dot(lax.all_gather(attended, 'rep', axis=0, tiled=True), out_proj, pr...]
    unnamed x21 -> x1, local copies, waits for them, and re-layouts: 14.4 us -> 1.31 us
    all_to_all x1 -> x0, waiting for transfers between devices: 4.82 us -> none  [per_device(): lax.all_to_all(partial_cols.astype(jnp.bfloat16), 'rep', split_axis=0, co...]
    all_to_all x1 -> x0, starting transfers between devices: 4.72 us -> none  [per_device(): lax.all_to_all(partial_cols.astype(jnp.bfloat16), 'rep', split_axis=0, co...]
  transfers between devices with their start and end apart: 3 -> 0, of which waited for: 3 -> 0; matrix products, arithmetic and copies ran while one was open for 1% -> 0% of each run, Pallas kernels for 0% -> 0%
where the time goes in v1:
time: 33.3 us; the launch traced here: 33.1 us
  Pallas kernels  31.8 us (95%)
  local copies, waits for them, and re-layouts  1.31 us (4%)
    pallas_call x1, Pallas kernels, fused_device(): pl.pallas_call(fused_kernel, out_shape=jax.ShapeDtypeStruct(residual.shap...  31.8 us
    unnamed x1, local copies, waits for them, and re-layouts  1.31 us

profile of v1, /device:TPU:0, one launch (start us, length us, event | category | flops | bytes accessed | tf_op | source)
XLA Modules:
  0.0 33.1 jit_solution(8029308439739751303)
XLA Ops:
  0.0 31.8 %shard_map.145 = bf16[4,1280]{1,0:T(4,128)(2,1)} custom-call(bf16[4,24,128]{2,1,0:T(8,128)(2,1)} %queries.1, bf16[4,2,128,128]{3,2,1,0:T(8,128)(2,1)} %cache_keys.1, bf16[4,2,128,128]{3,2,1,0:T(8,128)(2,1)} %cache_values.1, bf16[4,2,128]{2,1,0:T(2,128)(2,1)} %new_keys.1, bf16[4,2,128]{2,1,0:T(2,128)(2,1)} %new_values.1, bf16[4,1280]{1,0:T(4,128)(2,1)} %residual.1, ...), custom_call_target="tpu_custom_call" | custom-call | tf_op jit(solution)/shard_map/pallas_call | solution.py:622
  31.8 1.3 %copy.17 = bf16[4,1280]{1,0:T(4,128)(2,1)} copy(bf16[4,1280]{1,0:T(4,128)(2,1)} %shard_map.145) | data formatting | bytes 20480

commit v2 on v1

--- a/solution.py
+++ b/solution.py
@@ -176,10 +176,10 @@
     gate_w,
     up_w,
     down_w,
-    lengths,
-    skips,
-    ids,
-    routes,
+    cache_lengths,
+    skip_flags,
+    expert_ids,
+    route_scores,
     out,
     q_v,
     k_v,
@@ -192,6 +192,10 @@
     gate_v,
     up_v,
     down_v,
+    lengths,
+    skips,
+    ids,
+    routes,
     att_f,
     att_all,
     att_wide,
@@ -213,7 +217,8 @@
     proj_send,
     proj_recv,
     mid_send,
-    fwd_send,
+    across_send,
+    beside_send,
     mid_recv,
     exp_send,
     exp_recv,
@@ -234,13 +239,18 @@
             device_id_type=MESH,
         )
 
+    across = lax.rem(h + 2, N)
+    beside = h + 1 - 2 * lax.rem(h, 2)
     barrier = pltpu.get_barrier_semaphore()
     for i in range(N):
-        for j in range(N):
-
-            @pl.when(jnp.logical_or(r != i, h != j))
-            def _():
-                pl.semaphore_signal(barrier, inc=1, device_id=(g, i, j), device_id_type=MESH)
+
+        @pl.when(r != i)
+        def _():
+            pl.semaphore_signal(barrier, inc=1, device_id=(g, i, h), device_id_type=MESH)
+
+        @pl.when(h != i)
+        def _():
+            pl.semaphore_signal(barrier, inc=1, device_id=(g, r, i), device_id_type=MESH)
 
     loads = [
         pltpu.make_async_copy(src, dst, load_sem.at[i])
@@ -256,6 +266,10 @@
                 (gate_w, gate_v),
                 (up_w, up_v),
                 (down_w, down_v),
+                (cache_lengths, lengths),
+                (skip_flags, skips),
+                (expert_ids, ids),
+                (route_scores, routes),
             )
         )
     ]
@@ -266,11 +280,7 @@
         )
         for c in range(N)
     ]
-    for copy in loads[:6]:
-        copy.start()
-    for copy in w_loads:
-        copy.start()
-    for copy in loads[6:]:
+    for copy in loads[10:] + loads[:6] + w_loads + loads[6:10]:
         copy.start()
 
     heads = q_v.shape[1]
@@ -303,6 +313,8 @@
         jnp.int32, (lines, blocks), 0
     ) // per_block == lax.broadcasted_iota(jnp.int32, (lines, blocks), 1)
     own = jnp.sum(jnp.where(own_here, own_wide, 0.0), axis=1, keepdims=True) * scaling
+    for copy in loads[10:]:
+        copy.wait()
     filled = lax.broadcasted_iota(jnp.int32, (lines, slots), 1) < by_row(
         (lines, slots), heads, lambda i: lengths[i]
     )
@@ -328,7 +340,7 @@
     res = res_v[...].astype(jnp.float32)
     res_pack[...] = pack_rows(res).astype(jnp.bfloat16)
 
-    pl.semaphore_wait(barrier, N * N - 1)
+    pl.semaphore_wait(barrier, 2 * (N - 1))
 
     def att_copy(i):
         return remote(att_all.at[r], att_all.at[r], att_send.at[i], att_recv.at[r], i, h)
@@ -336,11 +348,11 @@
     def att_arrival(i):
         return remote(att_all.at[i], att_all.at[i], att_send.at[i], att_recv.at[i], i, h)
 
-    def res_copy(j):
-        return remote(res_pack, res_in.at[r], res_send.at[j], res_recv.at[r], h, j)
+    def res_copy():
+        return remote(res_pack, res_in.at[r], res_send, res_recv.at[r], h, h)
 
     def res_arrival(i):
-        return remote(res_pack, res_in.at[i], res_send.at[i], res_recv.at[i], i, r)
+        return remote(res_pack, res_in.at[i], res_send, res_recv.at[i], i, h)
 
     for i in range(N):
 
@@ -348,11 +360,9 @@
         def _():
             att_copy(i).start()
 
-    for j in range(N):
-
-        @pl.when(jnp.logical_or(r != h, h != j))
-        def _():
-            res_copy(j).start()
+    @pl.when(r != h)
+    def _():
+        res_copy().start()
 
     @pl.when(r == h)
     def _():
@@ -367,14 +377,28 @@
     for t in range(per_quarter):
         cut = att_all[:, :, t * HEAD_SIZE : (t + 1) * HEAD_SIZE]
         att_wide[t] = cut.astype(jnp.float32).reshape(N * ALL, HEAD_SIZE)
-    total = None
+    @pl.when(r == h)
+    def _():
+        for i in range(N):
+
+            @pl.when(r != i)
+            def _():
+                res_arrival(i).wait_recv()
+
+    @pl.when(r != h)
+    def _():
+        res_in[...] = jnp.zeros_like(res_in)
+
+    total = jnp.concatenate(
+        [unpack_rows(res_in[i].astype(jnp.float32)) for i in range(N)], axis=0
+    )
     for c in range(N):
         w_loads[c].wait()
         lhs = jnp.concatenate(
             [att_wide[t, pl.ds(c, ALL, stride=N), :] for t in range(per_quarter)], axis=1
         ).astype(jnp.bfloat16)
         part = dot(lhs, w_v[pl.ds(c * depth, depth), :])
-        total = part if total is None else total + part
+        total = total + part
 
     def proj_copy(j):
         return remote(proj_out.at[j], proj_in.at[h], proj_send.at[j], proj_recv.at[h], r, j)
@@ -396,17 +420,6 @@
         def _():
             proj_in[j] = proj_out[j]
 
-    for i in range(N):
-
-        @pl.when(jnp.logical_or(r != h, r != i))
-        def _():
-            res_arrival(i).wait_recv()
-
-    res_all = [res_in[i].astype(jnp.float32) for i in range(N)]
-    middle = jnp.zeros((ALL, PIECE), jnp.float32)
-    for j in range(N):
-        mine = jnp.concatenate([x[ROWS * j : ROWS * (j + 1)] for x in res_all], axis=0)
-        middle = jnp.where(h == j, mine, middle)
     for j in range(N):
 
         @pl.when(h != j)
@@ -416,7 +429,7 @@
     summed = proj_in[0].astype(jnp.float32)
     for j in range(1, N):
         summed = summed + proj_in[j].astype(jnp.float32)
-    mid_all[r, h] = (middle + summed).astype(jnp.bfloat16)
+    mid_all[r, h] = summed.astype(jnp.bfloat16)
 
     def mid_copy(i):
         return remote(
@@ -425,45 +438,48 @@
 
     def mid_arrival(i, j):
         return remote(
-            mid_all.at[i, j], mid_all.at[i, j], mid_send.at[i], mid_recv.at[i, j], i, j
+            mid_all.at[i, j], mid_all.at[i, j], mid_send.at[0], mid_recv.at[i, j], r, beside
         )
 
-    def mid_forward(i, j):
+    def mid_across(i):
         return remote(
-            mid_all.at[i, h], mid_all.at[i, h], fwd_send.at[i, j], mid_recv.at[i, h], r, j
+            mid_all.at[i, h], mid_all.at[i, h], across_send.at[i], mid_recv.at[i, h], r, across
         )
 
+    def mid_beside(i, k):
+        j = (h, across)[k]
+        return remote(
+            mid_all.at[i, j],
+            mid_all.at[i, j],
+            beside_send.at[i, k],
+            mid_recv.at[i, j],
+            r,
+            beside,
+        )
+
     for i in range(N):
 
         @pl.when(r != i)
         def _():
             mid_copy(i).start()
 
-    for j in range(N):
-
-        @pl.when(h != j)
-        def _():
-            mid_forward(r, j).start()
-
-    for i in range(N):
-
-        @pl.when(r != i)
-        def _():
-            mid_arrival(i, h).wait_recv()
-            for j in range(N):
-
-                @pl.when(h != j)
-                def _():
-                    mid_forward(i, j).start()
-
+    mid_across(r).start()
+    mid_beside(r, 0).start()
+    for turn in range(1, N):
+        i = lax.rem(r + turn, N)
+        mid_arrival(i, h).wait_recv()
+        mid_across(i).start()
+        mid_beside(i, 0).start()
+    for turn in range(N):
+        i = lax.rem(r + turn, N)
+        mid_arrival(i, across).wait_recv()
+        mid_beside(i, 1).start()
     for i in range(6, 10):
         loads[i].wait()
-    for i in range(N):
-        for j in range(N):
-
-            @pl.when(h != j)
-            def _():
-                mid_arrival(i, j).wait_recv()
+    far = lax.rem(beside + 2, N)
+    for i in range(N):
+        mid_arrival(i, beside).wait_recv()
+        mid_arrival(i, far).wait_recv()
 
     rows = []
     squares = jnp.zeros((ALL, 1), jnp.float32)
@@ -575,12 +591,14 @@
         def _():
             proj_copy(i).wait_send()
             exp_copy(i).wait_send()
-            for k in range(N):
-                mid_forward(k, i).wait_send()
-
-        @pl.when(jnp.logical_or(r != h, h != i))
-        def _():
-            res_copy(i).wait_send()
+
+        mid_across(i).wait_send()
+        mid_beside(i, 0).wait_send()
+        mid_beside(i, 1).wait_send()
+
+    @pl.when(r != h)
+    def _():
+        res_copy().wait_send()
 
 
 def fused_device(
@@ -615,6 +633,7 @@
         up_w,
         down_w,
     )
+    scalars = (cache_lengths, skip_flags, expert_ids.T, route_scores.T)
     heads = queries.shape[1]
     columns = residual.shape[1]
     depth = heads * HEAD_SIZE // N
@@ -622,10 +641,10 @@
     return pl.pallas_call(
         fused_kernel,
         out_shape=jax.ShapeDtypeStruct(residual.shape, bf16),
-        in_specs=[pl.BlockSpec(memory_space=pl.ANY)] * len(inputs)
-        + [pl.BlockSpec(memory_space=pltpu.SMEM)] * 4,
+        in_specs=[pl.BlockSpec(memory_space=pl.ANY)] * (len(inputs) + len(scalars)),
         out_specs=pl.BlockSpec(memory_space=pltpu.VMEM),
         scratch_shapes=[pltpu.VMEM(x.shape, x.dtype) for x in inputs]
+        + [pltpu.SMEM(x.shape, x.dtype) for x in scalars]
         + [
             pltpu.VMEM((ROWS * heads, HEAD_SIZE), f32),
             pltpu.VMEM((N, ALL, depth), bf16),
@@ -639,16 +658,17 @@
             pltpu.VMEM((N, ALL, columns), bf16),
             pltpu.VMEM((N, ALL, PIECE), bf16),
             pltpu.VMEM((N, ALL, PIECE), bf16),
-            dma((10,)),
-            dma((N,)),
-            dma((N,)),
-            dma((N,)),
-            dma((N,)),
-            dma((N,)),
-            dma((N,)),
-            dma((N,)),
-            dma((N,)),
-            dma((N, N)),
+            dma((len(inputs) + len(scalars) - 1,)),
+            dma((N,)),
+            dma((N,)),
+            dma((N,)),
+            dma,
+            dma((N,)),
+            dma((N,)),
+            dma((N,)),
+            dma((N,)),
+            dma((N,)),
+            dma((N, 2)),
             dma((N, N)),
             dma((N,)),
             dma((N,)),
@@ -658,7 +678,7 @@
         compiler_params=pltpu.CompilerParams(
             collective_id=0, has_side_effects=True, vmem_limit_bytes=63 * 1024 * 1024
         ),
-    )(*inputs, cache_lengths, skip_flags, expert_ids.T, route_scores.T)
+    )(*inputs, *scalars)
 
 
 def solution(mesh):

time: 33.3 us -> 32.3 us (0.970)
  Pallas kernels: 31.8 us -> 30.8 us
    pallas_call x1, Pallas kernels: 31.8 us -> 30.8 us  [fused_device(): pl.pallas_call(fused_kernel, out_shape=jax.ShapeDtypeStruct(residual.shap...]
where the time goes in v2:
time: 32.3 us; the launch traced here: 32.1 us
  Pallas kernels  30.8 us (95%)
  local copies, waits for them, and re-layouts  1.31 us (4%)
    pallas_call x1, Pallas kernels, fused_device(): pl.pallas_call(fused_kernel, out_shape=jax.ShapeDtypeStruct(residual.shap...  30.8 us
    unnamed x1, local copies, waits for them, and re-layouts  1.31 us

profile of v2, /device:TPU:0, one launch (start us, length us, event | category | flops | bytes accessed | tf_op | source)
XLA Modules:
  0.0 32.1 jit_solution(3118889351769468610)
XLA Ops:
  0.0 30.8 %shard_map.145 = bf16[4,1280]{1,0:T(4,128)(2,1)} custom-call(bf16[4,24,128]{2,1,0:T(8,128)(2,1)} %queries.1, bf16[4,2,128,128]{3,2,1,0:T(8,128)(2,1)} %cache_keys.1, bf16[4,2,128,128]{3,2,1,0:T(8,128)(2,1)} %cache_values.1, bf16[4,2,128]{2,1,0:T(2,128)(2,1)} %new_keys.1, bf16[4,2,128]{2,1,0:T(2,128)(2,1)} %new_values.1, bf16[4,1280]{1,0:T(4,128)(2,1)} %residual.1, ...), custom_call_target="tpu_custom_call" | custom-call | tf_op jit(solution)/shard_map/pallas_call | solution.py:641
  30.8 1.3 %copy.17 = bf16[4,1280]{1,0:T(4,128)(2,1)} copy(bf16[4,1280]{1,0:T(4,128)(2,1)} %shard_map.145) | data formatting | bytes 20480

commit v3 on v2

--- a/solution.py
+++ b/solution.py
@@ -217,8 +217,6 @@
     proj_send,
     proj_recv,
     mid_send,
-    across_send,
-    beside_send,
     mid_recv,
     exp_send,
     exp_recv,
@@ -239,18 +237,11 @@
             device_id_type=MESH,
         )
 
-    across = lax.rem(h + 2, N)
-    beside = h + 1 - 2 * lax.rem(h, 2)
     barrier = pltpu.get_barrier_semaphore()
-    for i in range(N):
-
-        @pl.when(r != i)
-        def _():
-            pl.semaphore_signal(barrier, inc=1, device_id=(g, i, h), device_id_type=MESH)
-
-        @pl.when(h != i)
-        def _():
-            pl.semaphore_signal(barrier, inc=1, device_id=(g, r, i), device_id_type=MESH)
+    for turn in range(1, N * N):
+        to_rep = lax.rem(r + turn // N, N)
+        to_head = lax.rem(h + turn % N, N)
+        pl.semaphore_signal(barrier, inc=1, device_id=(g, to_rep, to_head), device_id_type=MESH)
 
     loads = [
         pltpu.make_async_copy(src, dst, load_sem.at[i])
@@ -340,7 +331,7 @@
     res = res_v[...].astype(jnp.float32)
     res_pack[...] = pack_rows(res).astype(jnp.bfloat16)
 
-    pl.semaphore_wait(barrier, 2 * (N - 1))
+    pl.semaphore_wait(barrier, N * N - 1)
 
     def att_copy(i):
         return remote(att_all.at[r], att_all.at[r], att_send.at[i], att_recv.at[r], i, h)
@@ -431,55 +422,28 @@
         summed = summed + proj_in[j].astype(jnp.float32)
     mid_all[r, h] = summed.astype(jnp.bfloat16)
 
-    def mid_copy(i):
+    def partner(turn):
+        return lax.rem(r + turn // N, N), lax.rem(h + turn % N, N)
+
+    def mid_copy(turn):
+        i, j = partner(turn)
         return remote(
-            mid_all.at[r, h], mid_all.at[r, h], mid_send.at[i], mid_recv.at[r, h], i, h
+            mid_all.at[r, h], mid_all.at[r, h], mid_send.at[turn], mid_recv.at[r, h], i, j
         )
 
-    def mid_arrival(i, j):
+    def mid_arrival(turn):
+        i, j = partner(turn)
         return remote(
-            mid_all.at[i, j], mid_all.at[i, j], mid_send.at[0], mid_recv.at[i, j], r, beside
+            mid_all.at[i, j], mid_all.at[i, j], mid_send.at[turn], mid_recv.at[i, j], i, j
         )
 
-    def mid_across(i):
-        return remote(
-            mid_all.at[i, h], mid_all.at[i, h], across_send.at[i], mid_recv.at[i, h], r, across
-        )
-
-    def mid_beside(i, k):
-        j = (h, across)[k]
-        return remote(
-            mid_all.at[i, j],
-            mid_all.at[i, j],
-            beside_send.at[i, k],
-            mid_recv.at[i, j],
-            r,
-            beside,
-        )
-
-    for i in range(N):
-
-        @pl.when(r != i)
-        def _():
-            mid_copy(i).start()
-
-    mid_across(r).start()
-    mid_beside(r, 0).start()
-    for turn in range(1, N):
-        i = lax.rem(r + turn, N)
-        mid_arrival(i, h).wait_recv()
-        mid_across(i).start()
-        mid_beside(i, 0).start()
-    for turn in range(N):
-        i = lax.rem(r + turn, N)
-        mid_arrival(i, across).wait_recv()
-        mid_beside(i, 1).start()
+    order = [N * i + j for i in (2, 1, 3, 0) for j in range(N) if i or j]
+    for turn in order:
+        mid_copy(turn).start()
     for i in range(6, 10):
         loads[i].wait()
-    far = lax.rem(beside + 2, N)
-    for i in range(N):
-        mid_arrival(i, beside).wait_recv()
-        mid_arrival(i, far).wait_recv()
+    for turn in range(1, N * N):
+        mid_arrival(turn).wait_recv()
 
     rows = []
     squares = jnp.zeros((ALL, 1), jnp.float32)
@@ -584,7 +548,6 @@
         @pl.when(r != i)
         def _():
             att_copy(i).wait_send()
-            mid_copy(i).wait_send()
             back_copy(i).wait_send()
 
         @pl.when(h != i)
@@ -592,10 +555,8 @@
             proj_copy(i).wait_send()
             exp_copy(i).wait_send()
 
-        mid_across(i).wait_send()
-        mid_beside(i, 0).wait_send()
-        mid_beside(i, 1).wait_send()
-
+    for turn in range(1, N * N):
+        mid_copy(turn).wait_send()
     @pl.when(r != h)
     def _():
         res_copy().wait_send()
@@ -666,9 +627,7 @@
             dma((N,)),
             dma((N,)),
             dma((N,)),
-            dma((N,)),
-            dma((N,)),
-            dma((N, 2)),
+            dma((N * N,)),
             dma((N, N)),
             dma((N,)),
             dma((N,)),

time: 32.3 us -> 31.7 us (0.981)
  Pallas kernels: 30.8 us -> 30.2 us
    pallas_call x1, Pallas kernels: 30.8 us -> 30.2 us  [fused_device(): pl.pallas_call(fused_kernel, out_shape=jax.ShapeDtypeStruct(residual.shap...]
where the time goes in v3:
time: 31.7 us; the launch traced here: 31.5 us
  Pallas kernels  30.2 us (95%)
  local copies, waits for them, and re-layouts  1.31 us (4%)
    pallas_call x1, Pallas kernels, fused_device(): pl.pallas_call(fused_kernel, out_shape=jax.ShapeDtypeStruct(residual.shap...  30.2 us
    unnamed x1, local copies, waits for them, and re-layouts  1.31 us

profile of v3, /device:TPU:0, one launch (start us, length us, event | category | flops | bytes accessed | tf_op | source)
XLA Modules:
  0.0 31.5 jit_solution(9334020563850111311)
XLA Ops:
  0.0 30.2 %shard_map.145 = bf16[4,1280]{1,0:T(4,128)(2,1)} custom-call(bf16[4,24,128]{2,1,0:T(8,128)(2,1)} %queries.1, bf16[4,2,128,128]{3,2,1,0:T(8,128)(2,1)} %cache_keys.1, bf16[4,2,128,128]{3,2,1,0:T(8,128)(2,1)} %cache_values.1, bf16[4,2,128]{2,1,0:T(2,128)(2,1)} %new_keys.1, bf16[4,2,128]{2,1,0:T(2,128)(2,1)} %new_values.1, bf16[4,1280]{1,0:T(4,128)(2,1)} %residual.1, ...), custom_call_target="tpu_custom_call" | custom-call | tf_op jit(solution)/shard_map/pallas_call | solution.py:602
  30.2 1.3 %copy.17 = bf16[4,1280]{1,0:T(4,128)(2,1)} copy(bf16[4,1280]{1,0:T(4,128)(2,1)} %shard_map.145) | data formatting | bytes 20480

commit v4 on v3

--- a/solution.py
+++ b/solution.py
@@ -204,8 +204,6 @@
     proj_out,
     proj_in,
     mid_all,
-    exp_out,
-    exp_in,
     back_out,
     back_in,
     load_sem,
@@ -218,8 +216,6 @@
     proj_recv,
     mid_send,
     mid_recv,
-    exp_send,
-    exp_recv,
     back_send,
     back_recv,
 ):
@@ -464,22 +460,38 @@
         up = up + dot(normed, up_v[0, cut, :])
     hidden = (gate / (1.0 + jnp.exp(-gate)) * up).astype(jnp.bfloat16)
 
-    def exp_copy(j):
-        return remote(exp_out.at[j], exp_in.at[h], exp_send.at[j], exp_recv.at[h], r, j)
-
-    def exp_arrival(j):
-        return remote(exp_out.at[j], exp_in.at[j], exp_send.at[j], exp_recv.at[j], r, j)
+    def back_copy(turn):
+        i, j = partner(turn)
+        return remote(
+            back_out.at[i, j], back_in.at[r, h], back_send.at[turn], back_recv.at[r, h], i, j
+        )
+
+    def back_arrival(turn):
+        i, j = partner(turn)
+        return remote(
+            back_out.at[i, j], back_in.at[i, j], back_send.at[turn], back_recv.at[i, j], i, j
+        )
 
     for j in range(N):
-        exp_out[j] = dot(hidden, down_v[0, :, pl.ds(j * columns, columns)]).astype(jnp.bfloat16)
-
-        @pl.when(h != j)
-        def _():
-            exp_copy(j).start()
-
-        @pl.when(h == j)
-        def _():
-            exp_in[j] = exp_out[j]
+        part = dot(hidden, down_v[0, :, pl.ds(j * columns, columns)])
+        for i in range(N):
+            back_out[i, j] = pack_rows(part[ROWS * i : ROWS * (i + 1)]).astype(jnp.bfloat16)
+        turned = lax.rem(j - h + N, N)
+        for away in (2, 1, 3, 0):
+            i = lax.rem(r + away, N)
+            copy = remote(
+                back_out.at[i, j],
+                back_in.at[r, h],
+                back_send.at[away * N + turned],
+                back_recv.at[r, h],
+                i,
+                j,
+            )
+            if away:
+                copy.start()
+            else:
+                pl.when(h != j)(copy.start)
+    back_in[r, h] = back_out[r, h]
 
     line = lax.broadcasted_iota(jnp.int32, (ROWS, ALL), 1)
     want = lax.broadcasted_iota(jnp.int32, (ROWS, ALL), 0) + r * ROWS
@@ -504,42 +516,15 @@
         sum(jnp.where(named[k] == e, shares[k], 0.0) for k in range(top)) for e in range(N)
     ]
 
-    for j in range(N):
-
-        @pl.when(h != j)
-        def _():
-            exp_arrival(j).wait_recv()
-
-    expert = exp_in[0].astype(jnp.float32)
-    for j in range(1, N):
-        expert = expert + exp_in[j].astype(jnp.float32)
-
-    def back_copy(i):
-        return remote(back_out.at[i], back_in.at[r], back_send.at[i], back_recv.at[r], i, h)
-
-    def back_arrival(i):
-        return remote(back_out.at[i], back_in.at[i], back_send.at[i], back_recv.at[i], i, h)
-
-    for i in range(N):
-        back_out[i] = pack_rows(expert[ROWS * i : ROWS * (i + 1)]).astype(jnp.bfloat16)
-
-        @pl.when(r != i)
-        def _():
-            back_copy(i).start()
-
-        @pl.when(r == i)
-        def _():
-            back_in[i] = back_out[i]
-
-    for i in range(N):
-
-        @pl.when(r != i)
-        def _():
-            back_arrival(i).wait_recv()
-
-    mixed = weights[0] * back_in[0].astype(jnp.float32)
-    for e in range(1, N):
-        mixed = mixed + weights[e] * back_in[e].astype(jnp.float32)
+    for turn in range(1, N * N):
+        back_arrival(turn).wait_recv()
+
+    mixed = jnp.zeros(packed, jnp.float32)
+    for e in range(N):
+        expert = back_in[e, 0].astype(jnp.float32)
+        for j in range(1, N):
+            expert = expert + back_in[e, j].astype(jnp.float32)
+        mixed = mixed + weights[e] * expert
     skipped = by_row((ROWS, columns), 1, lambda i: skips[i])
     out[...] = jnp.where(skipped == 0, own_mid + unpack_rows(mixed), res).astype(jnp.bfloat16)
 
@@ -548,15 +533,14 @@
         @pl.when(r != i)
         def _():
             att_copy(i).wait_send()
-            back_copy(i).wait_send()
 
         @pl.when(h != i)
         def _():
             proj_copy(i).wait_send()
-            exp_copy(i).wait_send()
 
     for turn in range(1, N * N):
         mid_copy(turn).wait_send()
+        back_copy(turn).wait_send()
     @pl.when(r != h)
     def _():
         res_copy().wait_send()
@@ -615,10 +599,8 @@
             pltpu.VMEM((N, ALL, PIECE), bf16),
             pltpu.VMEM((N, ALL, PIECE), bf16),
             pltpu.VMEM((N, N, ALL, PIECE), bf16),
-            pltpu.VMEM((N, ALL, columns), bf16),
-            pltpu.VMEM((N, ALL, columns), bf16),
-            pltpu.VMEM((N, ALL, PIECE), bf16),
-            pltpu.VMEM((N, ALL, PIECE), bf16),
+            pltpu.VMEM((N, N, ALL, PIECE), bf16),
+            pltpu.VMEM((N, N, ALL, PIECE), bf16),
             dma((len(inputs) + len(scalars) - 1,)),
             dma((N,)),
             dma((N,)),
@@ -629,10 +611,8 @@
             dma((N,)),
             dma((N * N,)),
             dma((N, N)),
-            dma((N,)),
-            dma((N,)),
-            dma((N,)),
-            dma((N,)),
+            dma((N * N,)),
+            dma((N, N)),
         ],
         compiler_params=pltpu.CompilerParams(
             collective_id=0, has_side_effects=True, vmem_limit_bytes=63 * 1024 * 1024

time: 31.7 us -> 30.3 us (0.956)
  the two profiles are of different devices: /device:TPU:0 before, /device:TPU:3 now
where the time goes in v4:
time: 30.3 us; the launch traced here: 30.1 us
  Pallas kernels  28.8 us (95%)
  local copies, waits for them, and re-layouts  1.31 us (4%)
    pallas_call x1, Pallas kernels, fused_device(): pl.pallas_call(fused_kernel, out_shape=jax.ShapeDtypeStruct(residual.shap...  28.8 us
    unnamed x1, local copies, waits for them, and re-layouts  1.31 us

profile of v4, /device:TPU:3, one launch (start us, length us, event | category | flops | bytes accessed | tf_op | source)
XLA Modules:
  0.0 30.1 jit_solution(8335411337952348128)
XLA Ops:
  0.0 28.8 %shard_map.145 = bf16[4,1280]{1,0:T(4,128)(2,1)} custom-call(bf16[4,24,128]{2,1,0:T(8,128)(2,1)} %queries.1, bf16[4,2,128,128]{3,2,1,0:T(8,128)(2,1)} %cache_keys.1, bf16[4,2,128,128]{3,2,1,0:T(8,128)(2,1)} %cache_values.1, bf16[4,2,128]{2,1,0:T(2,128)(2,1)} %new_keys.1, bf16[4,2,128]{2,1,0:T(2,128)(2,1)} %new_values.1, bf16[4,1280]{1,0:T(4,128)(2,1)} %residual.1, ...), custom_call_target="tpu_custom_call" | custom-call | tf_op jit(solution)/shard_map/pallas_call | solution.py:586
  28.8 1.3 %copy.17 = bf16[4,1280]{1,0:T(4,128)(2,1)} copy(bf16[4,1280]{1,0:T(4,128)(2,1)} %shard_map.145) | data formatting | bytes 20480
